TPU v7x, 32 devices: a whole 2x2x4 slice. The times are simulated.
32 devices in a mesh: groups: 2 (over x), seq: 8 (over z, y), tensor: 2 (over core).
Axes of the slice: x: 2, y: 2, z: 4, core: 2. Of those that a mesh axis runs over, the one named last changes fastest.
Arguments:
- enc_rows: bfloat16 [5120, 4096], P(('groups', 'seq')), parts along dimension 0, may hold values from -6 to 6
- enc_owner: int32 [5120], P(('groups', 'seq')), parts along dimension 0, may hold values from 0 to 7, as said below
- enc_doc: int32 [5120], P(('groups', 'seq')), parts along dimension 0, may hold values from 0 to 63, as said below
- dec_doc: int32 [4096], P(('groups', 'seq')), parts along dimension 0, may hold values from 0 to 63, as said below
- queries: bfloat16 [4096, 2048], P(('groups', 'seq'), 'tensor'), parts along dimension 0, may hold values from -120 to 120
- key_weight: bfloat16 [4096, 2048], P('seq', 'tensor'), may hold values from -0.09375 to 0.09375
- value_weight: bfloat16 [4096, 2048], P('seq', 'tensor'), may hold values from -0.09375 to 0.09375
- out_weight: bfloat16 [2048, 4096], P('tensor', 'seq'), may hold values from -0.125 to 0.125
Outputs:
- mixed: bfloat16 [4096, 4096], P(('groups', 'seq'), 'tensor'), parts along dimension 0
There are 2 independent parts, one for each index of `groups`. A program takes and returns all parts, laid end to end along the dimension named above; an argument that names none is the same for every part. Nothing has to cross between parts.
Inputs may be any that keep to these rules, and one draw needn't show every extreme that they name: `enc_owner`: the rows of one seq device fall into aligned blocks of 80 rows, all rows of a block with one destination; the blocks of one device have different destinations, and its first block's destination is the device itself. `enc_doc`: each document's encoder rows are a run inside one such block; a block holds one or two documents. `dec_doc`: every decoder token's document has encoder rows, and all of them have the token's own seq device as destination; a document's decoder tokens stand in one run.
All inputs are finite; a program needn't handle non-finite values.
Results may differ from a plain program's by a relative error of at most 0.011.
Values may be sent and summed in bfloat16 or wider, within the bound.
A program may use at most 128 MiB of HBM per device.

v0:
```python
import math

import jax
import jax.numpy as jnp
from jax import lax
from jax.sharding import PartitionSpec as P

HEAD = 256


def project_pair(source_rows, key_weight, value_weight):
    key_sums = jnp.dot(
        source_rows,
        lax.all_gather(key_weight, "seq", axis=0, tiled=True),
        preferred_element_type=jnp.float32,
    )
    value_sums = jnp.dot(
        source_rows,
        lax.all_gather(value_weight, "seq", axis=0, tiled=True),
        preferred_element_type=jnp.float32,
    )
    return (key_sums.astype(jnp.bfloat16), value_sums.astype(jnp.bfloat16))


def pack_blocks(payload, enc_owner, enc_doc, shard_count, block_rows):
    block_count = payload.shape[0] // block_rows
    lead_owner = enc_owner.reshape(block_count, block_rows)[:, 0]
    targets = jnp.arange(shard_count, dtype=jnp.int32)
    selector = lead_owner[None, :] == targets[:, None]
    flattened = payload.reshape(block_count, block_rows * payload.shape[1])
    packed = jnp.dot(
        selector.astype(payload.dtype), flattened, preferred_element_type=jnp.float32
    ).astype(payload.dtype)
    doc_blocks = enc_doc.reshape(block_count, block_rows) + 1
    packed_docs = jnp.sum(jnp.where(selector[:, :, None], doc_blocks[None, :, :], 0), axis=1) - 1
    return (packed.reshape(shard_count, block_rows, payload.shape[1]), packed_docs)


def on_device(enc_rows, enc_owner, enc_doc, dec_doc, queries, key_weight, value_weight, out_weight):
    shard_count = lax.axis_size("seq")
    block_rows = 2 * enc_rows.shape[0] // shard_count
    packed, packed_docs = pack_blocks(enc_rows, enc_owner, enc_doc, shard_count, block_rows)
    arrived, slot_docs = (
        lax.all_to_all(packed, "seq", split_axis=0, concat_axis=0, tiled=True),
        lax.all_to_all(packed_docs, "seq", split_axis=0, concat_axis=0, tiled=True),
    )
    arrived = arrived.reshape(shard_count * block_rows, enc_rows.shape[1])
    keys_here, values_here = project_pair(arrived, key_weight, value_weight)
    slot_docs = slot_docs.reshape(shard_count * block_rows)
    token_count = queries.shape[0]
    head_count = queries.shape[1] // HEAD
    query_heads = queries.reshape(token_count, head_count, HEAD)
    key_heads = keys_here.reshape(shard_count * block_rows, head_count, HEAD)
    value_heads = values_here.reshape(shard_count * block_rows, head_count, HEAD)
    score_scale = 1.0 / math.sqrt(HEAD)
    scores = (
        jnp.einsum("qhd,khd->hqk", query_heads, key_heads, preferred_element_type=jnp.float32)
        * score_scale
    )
    matching = dec_doc[:, None] == slot_docs[None, :]
    scores = jnp.where(matching[None, :, :], scores, -1e30)
    row_peak = jnp.max(scores, axis=2, keepdims=True)
    exponent = jnp.exp(scores - row_peak)
    probs = (exponent / jnp.sum(exponent, axis=2, keepdims=True)).astype(jnp.bfloat16)
    attended = jnp.einsum("hqk,khd->qhd", probs, value_heads, preferred_element_type=jnp.float32)
    attended = attended.astype(jnp.bfloat16).reshape(token_count, head_count * HEAD)
    partial_rows = jnp.dot(
        attended,
        lax.all_gather(out_weight, "seq", axis=1, tiled=True),
        preferred_element_type=jnp.float32,
    )
    return lax.psum_scatter(
        partial_rows.astype(jnp.bfloat16), "tensor", scatter_dimension=1, tiled=True
    )


def solution(mesh):
    return jax.shard_map(
        on_device,
        mesh=mesh,
        in_specs=(
            P(("groups", "seq"), None),
            P(("groups", "seq")),
            P(("groups", "seq")),
            P(("groups", "seq")),
            P(("groups", "seq"), "tensor"),
            P("seq", "tensor"),
            P("seq", "tensor"),
            P("tensor", "seq"),
        ),
        out_specs=P(("groups", "seq"), "tensor"),
        check_vma=False,
    )
```

profile of v0, /device:TPU:0, one launch (start us, length us, event | category | flops | bytes accessed | tf_op | source)
XLA Modules:
  0.0 510.9 jit_solution(9034970542907747312)
XLA Ops:
  6.5 0.0 copy-start.2
  6.5 0.0 copy-start.3
  6.5 0.0 all-gather.4.cloned.1.call-start
  6.5 0.7 all-gather.4.cloned.1.call-update
  7.3 0.0 all-gather.6.cloned.1.call-start
  7.3 0.7 all-gather.6.cloned.1.call-update
  8.0 0.0 all-gather.8.cloned.1.call-start
  8.1 0.7 all-gather.8.cloned.1.call-update
  8.7 0.0 copy-done.2
  8.8 0.1 reshape.96
  8.8 0.0 copy-done.3
  8.8 0.1 add.26
  8.9 0.1 slice_reduce_fusion
  9.0 0.1 iota_compare_fusion
  9.1 0.1 select_reduce_fusion
  9.2 0.6 broadcast_add_fusion
  9.8 7.3 %all-to-all-start.1 = ((s32[8,1,80]{2,1,0:T(1,128)}), s32[8,1,80]{2,1,0:T(1,128)S(1)}, u32[]{:S(2)}, u32[]{:S(2)}) async-start(s32[8,1,80]{2,1,0:T(1,128)} %bitcast.4), calls=%async_computation.1 | async-start | bytes 8192 | tf_op jit(solution)/shard_map/all_to_all | solution.py:45
  17.1 3.8 reshape.97
  20.9 2.2 convolution_convert_fusion
  23.1 5.2 %copy.28 = bf16[8,80,4096]{2,1,0:T(8,128)(2,1)} copy(bf16[8,80,4096]{2,0,1:T(8,128)(2,1)S(1)} %bitcast.48) | data formatting | bytes 10485760 | tf_op jit(solution)/shard_map/reshape | solution.py:36
  28.2 0.0 copy-start.4
  28.2 0.0 all-to-all-done.1
  28.2 6.1 %all-to-all-start = ((bf16[8,80,4096]{2,1,0:T(8,128)(2,1)}), bf16[8,80,4096]{2,1,0:T(8,128)(2,1)}, u32[]{:S(2)}, u32[]{:S(2)}) async-start(bf16[8,80,4096]{2,1,0:T(8,128)(2,1)} %copy.28), calls=%async_computation | async-start | bytes 10485760 | tf_op jit(solution)/shard_map/all_to_all | solution.py:44
  34.4 0.2 reduce-scatter.2.cloned.1.call-start
  34.6 0.5 broadcast.56
  35.1 0.7 reduce.5
  35.8 0.1 eq.43
  35.8 0.0 copy-done.4
  35.8 0.2 broadcast_compare_fusion
  36.0 196.6 %all-to-all-done = bf16[8,80,4096]{2,1,0:T(8,128)(2,1)} async-done(((bf16[8,80,4096]{2,1,0:T(8,128)(2,1)}), bf16[8,80,4096]{2,1,0:T(8,128)(2,1)}, u32[]{:S(2)}, u32[]{:S(2)}) %all-to-all-start) | async-done | bytes 5242912 | tf_op jit(solution)/shard_map/all_to_all | solution.py:44
  232.6 6.6 %all-gather.4.cloned.1.call-done = bf16[4096,1024]{1,0:T(8,128)(2,1)} async-done(((bf16[512,1024]{1,0:T(8,128)(2,1)}), bf16[4096,1024]{1,0:T(8,128)(2,1)}) %all-gather.4.cloned.1.call-update) | async-done | bytes 8388624 | tf_op jit(solution)/shard_map/all_gather | solution.py:19
  239.2 9.5 %convolution_convert_fusion.3 = bf16[640,1024]{1,0:T(8,128)(2,1)S(1)} fusion(bf16[640,4096]{1,0:T(8,128)(2,1)} %bitcast.1, bf16[4096,1024]{1,0:T(8,128)(2,1)} %all-gather.4.cloned.1.call-done), kind=kOutput, calls=%fused_computation.8 | convolution fusion | flops 5369364480 | bytes 14942208 | tf_op jit(solution)/shard_map/dot_general | solution.py:17
  248.7 1.5 copy.35
  250.2 0.0 copy-start.1
  250.2 113.4 %all-gather.6.cloned.1.call-done = bf16[4096,1024]{1,0:T(8,128)(2,1)} async-done(((bf16[512,1024]{1,0:T(8,128)(2,1)}), bf16[4096,1024]{1,0:T(8,128)(2,1)}) %all-gather.6.cloned.1.call-update) | async-done | bytes 8388624 | tf_op jit(solution)/shard_map/all_gather | solution.py:14
  363.6 9.5 %convolution_convert_fusion.2 = bf16[640,1024]{1,0:T(8,128)(2,1)S(1)} fusion(bf16[640,4096]{1,0:T(8,128)(2,1)} %bitcast.1, bf16[4096,1024]{1,0:T(8,128)(2,1)} %all-gather.6.cloned.1.call-done), kind=kOutput, calls=%fused_computation.7 | convolution fusion | flops 5369364480 | bytes 14942208 | tf_op jit(solution)/shard_map/dot_general | solution.py:12
  373.1 0.0 copy-start
  373.1 1.1 copy-done
  374.2 0.0 copy-done.1
  374.3 0.5 fusion.2
  374.8 2.5 fusion.27
  377.3 2.4 fusion.9
  379.7 109.5 %all-gather.8.cloned.1.call-done = bf16[1024,4096]{1,0:T(8,128)(2,1)} async-done(((bf16[1024,512]{1,0:T(8,128)(2,1)}), bf16[1024,4096]{1,0:T(8,128)(2,1)}) %all-gather.8.cloned.1.call-update) | async-done | bytes 8388624 | tf_op jit(solution)/shard_map/all_gather | solution.py:69
  489.2 7.1 %convolution_convert_fusion.1 = bf16[256,4096]{1,0:T(8,128)(2,1)} fusion(bf16[256,1024]{0,1:T(8,128)(2,1)S(1)} %bitcast.52, bf16[1024,4096]{1,0:T(8,128)(2,1)} %all-gather.8.cloned.1.call-done), kind=kOutput, calls=%fused_computation.2 | convolution fusion | flops 2148532224 | bytes 11010048 | tf_op jit(solution)/shard_map/dot_general | solution.py:67
  496.4 0.0 reduce-scatter.2.cloned.1.call-update
  496.4 8.0 %reduce-scatter.2.cloned.1.call-done = bf16[256,2048]{1,0:T(8,128)(2,1)} async-done(((bf16[256,4096]{1,0:T(8,128)(2,1)}), bf16[256,2048]{1,0:T(8,128)(2,1)}) %reduce-scatter.2.cloned.1.call-update) | async-done | bytes 1048592 | tf_op jit(solution)/shard_map/reduce_scatter | solution.py:72
  (1 shorter events, 0.0 us)
Async XLA Ops:
  6.5 2.2 copy-start.2
  6.5 2.3 copy-start.3
  6.5 232.7 %all-gather.4.cloned.1.call-start = ((), (), s32[]{:S(2)}) async-start(), calls=%async_computation.3 | async-start | bytes 9437184 | tf_op jit(solution)/shard_map/all_gather | solution.py:19
  7.3 356.3 %all-gather.6.cloned.1.call-start = ((), (), s32[]{:S(2)}) async-start(), calls=%async_computation.4 | async-start | bytes 9437184 | tf_op jit(solution)/shard_map/all_gather | solution.py:14
  8.0 481.2 %all-gather.8.cloned.1.call-start = ((), (), s32[]{:S(2)}) async-start(), calls=%async_computation.5 | async-start | bytes 9437184 | tf_op jit(solution)/shard_map/all_gather | solution.py:69
  9.8 18.4 %all-to-all-start.1 = ((s32[8,1,80]{2,1,0:T(1,128)}), s32[8,1,80]{2,1,0:T(1,128)S(1)}, u32[]{:S(2)}, u32[]{:S(2)}) async-start(s32[8,1,80]{2,1,0:T(1,128)} %bitcast.4), calls=%async_computation.1 | async-start | bytes 8192 | tf_op jit(solution)/shard_map/all_to_all | solution.py:45
  28.2 7.6 %copy-start.4 = (s32[256]{0:T(256)S(1)}, s32[256]{0:T(256)}, u32[]{:S(2)}) copy-start(s32[256]{0:T(256)} %param.11) | copy-start | bytes 3076
  28.2 204.4 %all-to-all-start = ((bf16[8,80,4096]{2,1,0:T(8,128)(2,1)}), bf16[8,80,4096]{2,1,0:T(8,128)(2,1)}, u32[]{:S(2)}, u32[]{:S(2)}) async-start(bf16[8,80,4096]{2,1,0:T(8,128)(2,1)} %copy.28), calls=%async_computation | async-start | bytes 10485760 | tf_op jit(solution)/shard_map/all_to_all | solution.py:44
  34.4 470.0 %reduce-scatter.2.cloned.1.call-start = ((), (), s32[]{:S(2)}) async-start(), calls=%async_computation.6 | async-start | bytes 3145728 | tf_op jit(solution)/shard_map/reduce_scatter | solution.py:72
  250.2 124.1 %copy-start.1 = (bf16[256,1024]{1,0:T(8,128)(2,1)S(1)}, bf16[256,1024]{1,0:T(8,128)(2,1)}, u32[]{:S(2)}) copy-start(bf16[256,1024]{1,0:T(8,128)(2,1)} %param.12) | copy-start | bytes 1572868
  373.1 1.2 copy-start
Sparse Core Ops, SparseCore 0:
  9.5 229.6 all-gather.3
  241.3 122.1 all-gather.5
  365.6 123.5 all-gather.7
  496.5 7.7 reduce-scatter.1
where the time goes:
time: 511 us
  waiting for transfers between devices  436 us (85%)
  matrix products  33.9 us (7%)
  starting transfers between devices  13.7 us (3%)
  between operations  13.2 us (3%)
  local copies, waits for them, and re-layouts  12.4 us (2%)
    all_to_all x1, waiting for transfers between devices, on_device(): lax.all_to_all(packed, 'seq', split_axis=0, concat_axis=0, tiled=True)  197 us
    all_gather x1, waiting for transfers between devices, project_pair(): lax.all_gather(key_weight, 'seq', axis=0, tiled=True)  113 us
    all_gather x1, waiting for transfers between devices, on_device(): lax.all_gather(out_weight, 'seq', axis=1, tiled=True)  110 us
  transfers between devices with their start and end apart: 6, of which 5 were waited for; matrix products, arithmetic and copies ran while one was open for 8% of the time, Pallas kernels for 0%

commit v1 on v0

v1 whole, which is shorter than its diff:
```python
import math

import jax
import jax.numpy as jnp
from jax import lax
from jax.sharding import PartitionSpec as P

HEAD = 256


def half_columns(weight):
    width = weight.shape[1] // lax.axis_size("groups")
    return lax.dynamic_slice_in_dim(weight, lax.axis_index("groups") * width, width, axis=1)


def gather_columns(weight):
    groups = lax.axis_size("groups")
    gathered = lax.all_gather(half_columns(weight), ("groups", "seq"), axis=0, tiled=True)
    return gathered.reshape(groups, gathered.shape[0] // groups, gathered.shape[1])


def project(rows, weight):
    parts = gather_columns(weight)
    return jnp.concatenate(
        [
            jnp.dot(rows, parts[g], preferred_element_type=jnp.float32).astype(jnp.bfloat16)
            for g in range(parts.shape[0])
        ],
        axis=1,
    )


def on_device(enc_rows, enc_owner, enc_doc, dec_doc, queries, key_weight, value_weight, out_weight):
    shard_count = lax.axis_size("seq")
    me = lax.axis_index("seq")
    tensors = lax.axis_size("tensor")
    block_rows = 2 * enc_rows.shape[0] // shard_count
    block_count = enc_rows.shape[0] // block_rows
    width = enc_rows.shape[1] // tensors
    payload = lax.dynamic_slice_in_dim(enc_rows, lax.axis_index("tensor") * width, width, axis=1)
    lead = enc_owner.reshape(block_count, block_rows)[:, 0]
    targets = jnp.arange(shard_count, dtype=jnp.int32)
    blocks = payload.reshape(block_count, block_rows, width)
    packed = jnp.zeros((shard_count, block_rows, width), payload.dtype)
    for b in range(block_count):
        packed = jnp.where((lead[b] == targets)[:, None, None], blocks[b][None], packed)
    arrived = lax.all_to_all(packed, "seq", split_axis=0, concat_axis=0, tiled=True)
    arrived = lax.all_gather(
        arrived.reshape(shard_count * block_rows, width), "tensor", axis=1, tiled=True
    )
    tags = lax.all_gather(jnp.stack([enc_owner, enc_doc]), "seq", axis=0)
    tags = tags.reshape(shard_count, 2, block_count, block_rows)
    slot_docs = jnp.sum(jnp.where(tags[:, 0] == me, tags[:, 1] + 1, 0), axis=1) - 1
    slot_docs = slot_docs.reshape(shard_count * block_rows)
    keys_here = project(arrived, key_weight)
    values_here = project(arrived, value_weight)
    token_count = queries.shape[0]
    head_count = queries.shape[1] // HEAD
    query_heads = queries.reshape(token_count, head_count, HEAD)
    key_heads = keys_here.reshape(shard_count * block_rows, head_count, HEAD)
    value_heads = values_here.reshape(shard_count * block_rows, head_count, HEAD)
    score_scale = 1.0 / math.sqrt(HEAD)
    scores = (
        jnp.einsum("qhd,khd->hqk", query_heads, key_heads, preferred_element_type=jnp.float32)
        * score_scale
    )
    matching = dec_doc[:, None] == slot_docs[None, :]
    scores = jnp.where(matching[None, :, :], scores, -1e30)
    row_peak = jnp.max(scores, axis=2, keepdims=True)
    exponent = jnp.exp(scores - row_peak)
    probs = (exponent / jnp.sum(exponent, axis=2, keepdims=True)).astype(jnp.bfloat16)
    attended = jnp.einsum("hqk,khd->qhd", probs, value_heads, preferred_element_type=jnp.float32)
    attended = attended.astype(jnp.bfloat16).reshape(token_count, head_count * HEAD)
    groups = lax.axis_size("groups")
    height = out_weight.shape[0] // groups
    mine = lax.dynamic_slice_in_dim(out_weight, lax.axis_index("groups") * height, height, axis=0)
    out_parts = lax.all_gather(mine, ("groups", "seq"), axis=0, tiled=False)
    out_parts = out_parts.reshape(groups, shard_count, height, out_weight.shape[1])
    partial_rows = sum(
        jnp.einsum(
            "tk,skn->tsn",
            attended[:, g * height : (g + 1) * height],
            out_parts[g],
            preferred_element_type=jnp.float32,
        )
        for g in range(groups)
    ).reshape(token_count, shard_count * out_weight.shape[1])
    return lax.psum_scatter(
        partial_rows.astype(jnp.bfloat16), "tensor", scatter_dimension=1, tiled=True
    )


def solution(mesh):
    return jax.shard_map(
        on_device,
        mesh=mesh,
        in_specs=(
            P(("groups", "seq"), None),
            P(("groups", "seq")),
            P(("groups", "seq")),
            P(("groups", "seq")),
            P(("groups", "seq"), "tensor"),
            P("seq", "tensor"),
            P("seq", "tensor"),
            P("tensor", "seq"),
        ),
        out_specs=P(("groups", "seq"), "tensor"),
        check_vma=False,
    )
```

time: 511 us -> 464 us (0.908)
  waiting for transfers between devices: 436 us -> 301 us
  blocking collectives: 0 us -> 97 us
  starting transfers between devices: 13.7 us -> 0.17 us
    all_to_all x2 -> x0, waiting for transfers between devices: 197 us -> none  [the longest x1 197 us: on_device(): lax.all_to_all(packed, 'seq', split_axis=0, concat_axis=0, tiled=True)]
    all_to_all x0 -> x1, blocking collectives: none -> 66.7 us  [on_device(): lax.all_to_all(packed, 'seq', split_axis=0, concat_axis=0, tiled=True)]
    all_gather x3 -> x4, waiting for transfers between devices: 229 us -> 293 us  [the longest x2 200 us: gather_columns(): lax.all_gather(half_columns(weight), ('groups', 'seq'), axis=0, tiled=True)]
    all_gather x0 -> x1, blocking collectives: none -> 30.4 us  [on_device(): tags = lax.all_gather(jnp.stack([enc_owner, enc_doc]), 'seq', axis=0)]
    all_to_all x2 -> x0, starting transfers between devices: 13.4 us -> none  [the longest x1 7.28 us: on_device(): lax.all_to_all(packed_docs, 'seq', split_axis=0, concat_axis=0, tiled=True)]
    reshape x4 -> x2, local copies, waits for them, and re-layouts: 10.5 us -> 0.95 us  [the longest x1 0.85 us: on_device(): lead = enc_owner.reshape(block_count, block_rows)[:, 0]]
    slice x1 -> x3, local copies, waits for them, and re-layouts: 0.11 us -> 5.74 us  [the longest x1 3.76 us: on_device(): out_parts[g]]
    dot_general x5 -> x6, matrix products: 29 us -> 27.3 us  [the longest x4 24.6 us: project(): jnp.dot(rows, parts[g], preferred_element_type=jnp.float32)]
  transfers between devices with their start and end apart: 6 -> 5, of which waited for: 5 -> 4; matrix products, arithmetic and copies ran while one was open for 8% -> 7% of each run, Pallas kernels for 0% -> 0%
where the time goes in v1:
time: 464 us
  waiting for transfers between devices  301 us (65%)
  blocking collectives  97 us (21%)
  matrix products  32.7 us (7%)
  local copies, waits for them, and re-layouts  14.7 us (3%)
  between operations  13.4 us (3%)
    all_gather x2, waiting for transfers between devices, gather_columns(): lax.all_gather(half_columns(weight), ('groups', 'seq'), axis=0, tiled=True)  200 us
    all_gather x1, waiting for transfers between devices, on_device(): out_parts = lax.all_gather(mine, ('groups', 'seq'), axis=0, tiled=False)  93.2 us
    all_to_all x1, blocking collectives, on_device(): lax.all_to_all(packed, 'seq', split_axis=0, concat_axis=0, tiled=True)  66.7 us
    all_gather x1, blocking collectives, on_device(): tags = lax.all_gather(jnp.stack([enc_owner, enc_doc]), 'seq', axis=0)  30.4 us
    dot_general x4, matrix products, project(): jnp.dot(rows, parts[g], preferred_element_type=jnp.float32)  24.6 us
  transfers between devices with their start and end apart: 5, of which 4 were waited for; matrix products, arithmetic and copies ran while one was open for 7% of the time, Pallas kernels for 0%

profile of v1, /device:TPU:0, one launch (start us, length us, event | category | flops | bytes accessed | tf_op | source)
XLA Modules:
  0.0 463.5 jit_solution(18229361801110235346)
XLA Ops:
  6.5 0.9 reshape.112
  7.4 0.6 fusion.43
  8.0 1.2 iota_compare_fusion
  9.1 1.3 iota_compare_fusion.2
  10.4 1.4 fusion.42
  11.9 0.7 select_select_fusion
  12.5 66.7 %all_to_all.5 = bf16[8,80,2048]{2,1,0:T(8,128)(2,1)} all-to-all(bf16[8,80,2048]{2,1,0:T(8,128)(2,1)S(1)} %select_select_fusion), channel_id=1, replica_groups=mesh['groups'=2,'seq'=8,'tensor'=2] {'seq'}, dimensions={0} | all-to-all | bytes 5242880 | tf_op jit(solution)/shard_map/all_to_all | solution.py:47
  79.2 0.0 all-gather.8.cloned.1.call-update
  79.2 0.0 copy-start.4
  79.2 0.0 copy-start.5
  79.2 0.0 copy-start.6
  79.3 0.0 all-gather.12.cloned.1.call-start
  79.3 0.8 constant_dynamic-slice_fusion.1
  80.1 0.0 all-gather.12.cloned.1.call-update
  80.2 0.0 all-gather.10.cloned.1.call-start
  80.2 0.4 copy-done.2
  80.6 0.9 constant_dynamic-slice_fusion.2
  81.5 0.0 all-gather.10.cloned.1.call-update
  81.5 0.0 all-gather.14.cloned.1.call-start
  81.5 0.8 constant_dynamic-slice_fusion
  82.4 0.0 all-gather.14.cloned.1.call-update
  82.4 0.0 reduce-scatter.2.cloned.1.call-start
  82.5 30.4 %all-gather.2 = s32[8,2,320]{2,1,0:T(2,128)S(1)} all-gather(s32[1,2,320]{2,1,0:T(2,128)S(1)} %add_bitcast_fusion), channel_id=2, replica_groups=mesh['groups'=2,'seq'=8,'tensor'=2] {'seq'}, dimensions={0}, use_global_device_ids=true | all-gather | bytes 23040 | tf_op jit(solution)/shard_map/all_gather | solution.py:51
  112.9 0.1 reshape.115
  113.0 0.1 sub.15
  113.1 0.2 broadcast_compare_fusion
  113.3 0.0 all-gather.8.cloned.1.call-done
  113.3 97.1 %all-gather.12.cloned.1.call-done = bf16[8192,512]{1,0:T(8,128)(2,1)} async-done(((bf16[512,512]{1,0:T(8,128)(2,1)}), bf16[8192,512]{1,0:T(8,128)(2,1)}) %all-gather.12.cloned.1.call-update) | async-done | bytes 8388624 | tf_op jit(solution)/shard_map/all_gather | solution.py:18
  210.4 7.3 %fusion.16 = bf16[640,512]{0,1:T(8,128)(2,1)S(1)} fusion(bf16[640,4096]{1,0:T(8,128)(2,1)} %all-gather.8.cloned.1.call-done, bf16[8192,512]{1,0:T(8,128)(2,1)} %all-gather.12.cloned.1.call-done), kind=kOutput, calls=%fused_computation.17 | convolution fusion | flops 2684682240 | bytes 10092544 | tf_op jit(solution)/shard_map/dot_general | solution.py:26
  217.8 0.3 copy-done.9
  218.0 3.4 fusion.19
  221.5 0.1 pad_maximum_fusion.1
  221.6 102.6 %all-gather.10.cloned.1.call-done = bf16[8192,512]{1,0:T(8,128)(2,1)} async-done(((bf16[512,512]{1,0:T(8,128)(2,1)}), bf16[8192,512]{1,0:T(8,128)(2,1)}) %all-gather.10.cloned.1.call-update) | async-done | bytes 8388624 | tf_op jit(solution)/shard_map/all_gather | solution.py:18
  324.2 7.3 %fusion.10 = bf16[640,512]{0,1:T(8,128)(2,1)S(1)} fusion(bf16[640,4096]{1,0:T(8,128)(2,1)} %all-gather.8.cloned.1.call-done, bf16[8192,512]{1,0:T(8,128)(2,1)} %all-gather.10.cloned.1.call-done), kind=kOutput, calls=%fused_computation.15 | convolution fusion | flops 2684682240 | bytes 10092544 | tf_op jit(solution)/shard_map/dot_general | solution.py:26
  331.6 6.5 %fusion.13 = bf16[640,512]{0,1:T(8,128)(2,1)S(1)} fusion(bf16[640,4096]{1,0:T(8,128)(2,1)} %all-gather.8.cloned.1.call-done, bf16[8192,512]{1,0:T(8,128)(2,1)S(1)} %copy-done.8), kind=kOutput, calls=%fused_computation.16 | convolution fusion | flops 2684682240 | bytes 10092544 | tf_op jit(solution)/shard_map/dot_general | solution.py:26
  338.1 0.0 copy-start.10
  338.1 1.2 pad_maximum_fusion
  339.3 2.7 fusion.44
  342.0 2.7 fusion.26
  344.7 93.2 %all-gather.14.cloned.1.call-done = bf16[8192,512]{1,0:T(8,128)(2,1)} async-done(((bf16[512,512]{1,0:T(8,128)(2,1)}), bf16[8192,512]{1,0:T(8,128)(2,1)}) %all-gather.14.cloned.1.call-update) | async-done | bytes 8388624 | tf_op jit(solution)/shard_map/all_gather | solution.py:77
  437.9 3.8 fusion.41
  441.7 1.3 fusion.30
  443.0 1.3 add_convert_fusion
  444.3 0.0 copy-start.1
  444.3 2.4 copy.26
  446.8 0.0 reduce-scatter.2.cloned.1.call-update
  446.8 8.0 %reduce-scatter.2.cloned.1.call-done = bf16[256,2048]{0,1:T(8,128)(2,1)} async-done(((bf16[256,4096]{0,1:T(8,128)(2,1)}), bf16[256,2048]{0,1:T(8,128)(2,1)}) %reduce-scatter.2.cloned.1.call-update) | async-done | bytes 1048592 | tf_op jit(solution)/shard_map/reduce_scatter | solution.py:88
  454.7 2.3 copy.27
  (21 shorter events, 0.1 us)
Async XLA Ops:
  6.5 72.8 %copy-start = (bf16[512,1024]{1,0:T(8,128)(2,1)S(1)}, bf16[512,1024]{1,0:T(8,128)(2,1)}, u32[]{:S(2)}) copy-start(bf16[512,1024]{1,0:T(8,128)(2,1)} %param.13) | copy-start | bytes 3145732
  6.5 106.8 %all-gather.8.cloned.1.call-start = ((), (), s32[]{:S(2)}) async-start(), calls=%async_computation.2 | async-start | bytes 7864320 | tf_op jit(solution)/shard_map/all_gather | solution.py:48
  79.2 1.4 copy-start.2
  79.2 2.3 copy-start.3
  79.2 3.2 copy-start.4
  79.2 3.2 copy-start.5
  79.2 33.9 %copy-start.6 = (s32[256]{0:T(256)S(1)}, s32[256]{0:T(256)}, u32[]{:S(2)}) copy-start(s32[256]{0:T(256)} %param.11) | copy-start | bytes 3076
  79.3 131.2 %all-gather.12.cloned.1.call-start = ((), (), s32[]{:S(2)}) async-start(), calls=%async_computation.4 | async-start | bytes 8912896 | tf_op jit(solution)/shard_map/all_gather | solution.py:18
  80.2 244.1 %all-gather.10.cloned.1.call-start = ((), (), s32[]{:S(2)}) async-start(), calls=%async_computation.3 | async-start | bytes 8912896 | tf_op jit(solution)/shard_map/all_gather | solution.py:18
  81.5 356.4 %all-gather.14.cloned.1.call-start = ((), (), s32[]{:S(2)}) async-start(), calls=%async_computation.6 | async-start | bytes 8912896 | tf_op jit(solution)/shard_map/all_gather | solution.py:77
  82.4 372.3 %reduce-scatter.2.cloned.1.call-start = ((), (), s32[]{:S(2)}) async-start(), calls=%async_computation.5 | async-start | bytes 3145728 | tf_op jit(solution)/shard_map/reduce_scatter | solution.py:88
  210.4 7.3 %copy-start.7 = (bf16[8192,512]{1,0:T(8,128)(2,1)S(1)}, bf16[8192,512]{1,0:T(8,128)(2,1)}, u32[]{:S(2)}) copy-start(bf16[8192,512]{1,0:T(8,128)(2,1)} %all-gather.12.cloned.1.call-done) | copy-start | bytes 25165828
  210.4 7.6 %copy-start.9 = (bf16[640,4096]{1,0:T(8,128)(2,1)S(1)}, bf16[640,4096]{1,0:T(8,128)(2,1)}, u32[]{:S(2)}) copy-start(bf16[640,4096]{1,0:T(8,128)(2,1)} %all-gather.8.cloned.1.call-done) | copy-start | bytes 15728644
  324.2 7.3 %copy-start.8 = (bf16[8192,512]{1,0:T(8,128)(2,1)S(1)}, bf16[8192,512]{1,0:T(8,128)(2,1)}, u32[]{:S(2)}) copy-start(bf16[8192,512]{1,0:T(8,128)(2,1)} %all-gather.10.cloned.1.call-done) | copy-start | bytes 25165828
  338.1 1.2 copy-start.10
  444.3 12.7 %copy-start.1 = (bf16[512,1024]{1,0:T(8,128)(2,1)S(1)}, bf16[512,1024]{1,0:T(8,128)(2,1)}, u32[]{:S(2)}) copy-start(bf16[512,1024]{1,0:T(8,128)(2,1)} %param.13) | copy-start | bytes 3145732
Sparse Core Ops, SparseCore 0:
  79.3 14.2 all-gather.7
  96.4 114.0 all-gather.11
  213.2 111.0 all-gather.9
  326.9 111.0 all-gather.13
  446.9 7.7 reduce-scatter.1

commit v2 on v1

v2 whole, which is shorter than its diff:
```python
import functools
import math

import jax
import jax.numpy as jnp
from jax import lax
from jax.experimental import pallas as pl
from jax.experimental.pallas import tpu as pltpu
from jax.sharding import PartitionSpec as P

HEAD = 256
MESH = pl.DeviceIdType.MESH


def when(condition, action):
    if condition is None:
        action()
    else:
        pl.when(condition)(action)


def exchange_kernel(
    shards, groups, tensors,
    x_ref, d_ref, k_ref, v_ref, o_ref,
    xg, dg, kg, vg, og,
    local_sem, x_send, x_recv, d_send, d_recv, t_send, t_recv,
    up_send, down_send, side_send, cross_send, recv,
):
    layers = shards // 2
    me = lax.axis_index("seq")
    group = lax.axis_index("groups")
    core = lax.axis_index("tensor")
    layer, side = me // 2, lax.rem(me, 2)
    to_group = {"groups": 1 - group}
    to_core = {"tensor": 1 - core}

    barrier = pltpu.get_barrier_semaphore()
    for j in range(1, shards):
        pl.semaphore_signal(
            barrier, inc=1, device_id={"seq": lax.rem(me + j, shards)}, device_id_type=MESH
        )
    pl.semaphore_signal(barrier, inc=1, device_id=to_group, device_id_type=MESH)
    pl.semaphore_signal(barrier, inc=1, device_id=to_core, device_id_type=MESH)
    pl.semaphore_wait(barrier, shards + 1)

    finish = []
    width = x_ref.shape[2]
    columns = pl.ds(pl.multiple_of(core * width, 128), width)

    def send(condition, make):
        when(condition, lambda: make().start())
        finish.append((condition, lambda: make().wait_send()))

    def remote(src, dst, send_sem, recv_sem, device):
        return pltpu.make_async_remote_copy(
            src_ref=src, dst_ref=dst, send_sem=send_sem, recv_sem=recv_sem,
            device_id=device, device_id_type=MESH,
        )

    for j in range(1, shards):
        target = lax.rem(me + j, shards)

        def rows_copy(target=target):
            return remote(
                x_ref.at[target], xg.at[me, :, columns],
                x_send.at[target], x_recv.at[me], {"seq": target},
            )

        def docs_copy(target=target):
            return remote(
                d_ref.at[target], dg.at[me], d_send.at[target], d_recv.at[me], {"seq": target}
            )

        send(None, rows_copy)
        send(None, docs_copy)

    weights = ((k_ref, kg, 1), (v_ref, vg, 1), (o_ref, og, 0))

    def piece_of(which, cross, owner):
        ref, axis = weights[which][0], weights[which][2]
        extent = ref.shape[axis]
        plain = extent // 4
        length = (extent - plain) // 2
        if cross:
            cut = pl.ds(pl.multiple_of(plain + owner * length, 128), length)
        else:
            cut = pl.ds(0, plain)
        return (cut, slice(None)) if axis == 0 else (slice(None), cut)

    def forward(condition, which, cross, origin, own, send_sems, device, owner):
        ref, full, _ = weights[which]
        cut = piece_of(which, cross, owner)
        number = (which * 3 + (1 + owner if cross else 0)) * shards + origin
        slot = (which * 2 + cross) * shards + origin

        def make():
            source = ref.at[cut] if own else full.at[(origin,) + cut]
            return remote(
                source, full.at[(origin,) + cut], send_sems.at[slot], recv.at[number], device
            )

        send(condition, make)

    def arrive(condition, which, cross, origin, owner):
        ref, full, _ = weights[which]
        cut = piece_of(which, cross, owner)
        number = (which * 3 + (1 + owner if cross else 0)) * shards + origin

        def wait():
            remote(
                ref.at[cut], full.at[(origin,) + cut],
                cross_send.at[0], recv.at[number], to_group,
            ).wait_recv()

        when(condition, wait)

    def both(a, b):
        return b if a is None else jnp.logical_and(a, b)

    up = {"seq": me + 2}
    down = {"seq": me - 2}
    beside = {"seq": layer * 2 + 1 - side}
    can_up = layer + 1 < layers
    can_down = layer >= 1

    for which in range(3):
        for cross in (0, 1):
            forward(can_up, which, cross, me, True, up_send, up, group)
            forward(can_down, which, cross, me, True, down_send, down, group)
            forward(None, which, cross, me, True, side_send, beside, group)

    own_copies = [
        pltpu.make_async_copy(x_ref.at[me], xg.at[me, :, columns], local_sem.at[0]),
        pltpu.make_async_copy(d_ref.at[me], dg.at[me], local_sem.at[1]),
        pltpu.make_async_copy(k_ref, kg.at[me], local_sem.at[2]),
        pltpu.make_async_copy(v_ref, vg.at[me], local_sem.at[3]),
        pltpu.make_async_copy(o_ref, og.at[me], local_sem.at[4]),
    ]
    for copy in own_copies:
        copy.start()

    def own_rows():
        return remote(
            x_ref.at[me], xg.at[me, :, columns], t_send.at[me], t_recv.at[me], to_core
        )

    send(None, own_rows)

    def along(distance):
        for which in range(3):
            for cross in (0, 1):
                for sign in (-1, 1):
                    there = layer + sign * distance
                    origin = there * 2 + side
                    exists = there >= 0 if sign < 0 else there < layers
                    arrive(exists, which, cross, origin, group)
                    if sign < 0:
                        forward(
                            both(exists, can_up), which, cross, origin, False, up_send, up, group
                        )
                    else:
                        forward(
                            both(exists, can_down), which, cross, origin, False,
                            down_send, down, group,
                        )
                    forward(exists, which, cross, origin, False, side_send, beside, group)
                    if cross:
                        forward(exists, which, 1, origin, False, cross_send, to_group, group)

    def across(distance):
        for which in range(3):
            for cross in (0, 1):
                for sign in (-1, 1) if distance else (1,):
                    there = layer + sign * distance
                    origin = there * 2 + 1 - side
                    exists = None
                    if distance:
                        exists = there >= 0 if sign < 0 else there < layers
                    arrive(exists, which, cross, origin, group)
                    if cross:
                        forward(exists, which, 1, origin, False, cross_send, to_group, group)

    def pass_rows():
        for j in range(1, shards):
            source = lax.rem(me + shards - j, shards)
            remote(
                x_ref.at[source], xg.at[source, :, columns],
                x_send.at[source], x_recv.at[source], {"seq": source},
            ).wait_recv()

            def share(source=source):
                return remote(
                    xg.at[source, :, columns], xg.at[source, :, columns],
                    t_send.at[source], t_recv.at[source], to_core,
                )

            send(None, share)

    across(0)
    for distance in range(1, layers):
        along(distance)
        across(distance)
        if distance == 1:
            pass_rows()

    others = pl.ds(pl.multiple_of((1 - core) * width, 128), width)
    for j in range(shards):
        source = lax.rem(me + j, shards)
        remote(
            x_ref.at[source], xg.at[source, :, others],
            t_send.at[source], t_recv.at[source], to_core,
        ).wait_recv()
        if j:
            remote(
                d_ref.at[source], dg.at[source], d_send.at[source], d_recv.at[source],
                {"seq": source},
            ).wait_recv()
            for which in range(3):
                arrive(None, which, 1, source, 1 - group)
    for copy in own_copies:
        copy.wait()
    for condition, action in finish:
        when(condition, action)


def exchange(rows, docs, key_weight, value_weight, out_weight):
    shards, groups, tensors = (lax.axis_size(a) for a in ("seq", "groups", "tensor"))
    slot, width = rows.shape[1:]
    dma = pltpu.SemaphoreType.DMA
    any_space = pl.BlockSpec(memory_space=pl.ANY)
    return pl.pallas_call(
        functools.partial(exchange_kernel, shards, groups, tensors),
        out_shape=[
            jax.ShapeDtypeStruct((shards, slot, width * tensors), rows.dtype),
            jax.ShapeDtypeStruct(docs.shape, docs.dtype),
            *(
                jax.ShapeDtypeStruct((shards,) + w.shape, w.dtype)
                for w in (key_weight, value_weight, out_weight)
            ),
        ],
        in_specs=[any_space] * 5,
        out_specs=[any_space] * 5,
        scratch_shapes=[dma((5,))]
        + [dma((shards,))] * 6
        + [dma((6 * shards,))] * 4
        + [dma((9 * shards,))],
        compiler_params=pltpu.CompilerParams(collective_id=0, has_side_effects=True),
    )(rows, docs, key_weight, value_weight, out_weight)


def on_device(enc_rows, enc_owner, enc_doc, dec_doc, queries, key_weight, value_weight, out_weight):
    shard_count = lax.axis_size("seq")
    tensors = lax.axis_size("tensor")
    block_rows = 2 * enc_rows.shape[0] // shard_count
    block_count = enc_rows.shape[0] // block_rows
    slot = -(-block_rows // 16) * 16
    lanes = -(-slot // 128) * 128
    model = enc_rows.shape[1]
    width = model // tensors
    payload = lax.dynamic_slice_in_dim(enc_rows, lax.axis_index("tensor") * width, width, axis=1)
    lead = enc_owner.reshape(block_count, block_rows)[:, 0]
    targets = jnp.arange(shard_count, dtype=jnp.int32)
    blocks = payload.reshape(block_count, block_rows, width)
    blocks = jnp.pad(blocks, ((0, 0), (0, slot - block_rows), (0, 0)))
    doc_blocks = enc_doc.reshape(block_count, block_rows)
    doc_blocks = jnp.pad(doc_blocks, ((0, 0), (0, lanes - block_rows)), constant_values=-1)
    packed = jnp.zeros((shard_count, slot, width), payload.dtype)
    packed_docs = jnp.full((shard_count, lanes), -1, jnp.int32)
    for b in range(block_count):
        chosen = lead[b] == targets
        packed = jnp.where(chosen[:, None, None], blocks[b][None], packed)
        packed_docs = jnp.where(chosen[:, None], doc_blocks[b][None], packed_docs)
    packed_docs = jnp.broadcast_to(packed_docs[:, None, :], (shard_count, 8, lanes))
    arrived, slot_docs, key_full, value_full, out_full = exchange(
        packed, packed_docs, key_weight, value_weight, out_weight
    )
    slots = shard_count * slot
    arrived = arrived.reshape(slots, model)
    slot_docs = slot_docs[:, 0, :slot].reshape(slots)
    inner = key_weight.shape[1]
    keys_here = jnp.dot(
        arrived, key_full.reshape(model, inner), preferred_element_type=jnp.float32
    ).astype(jnp.bfloat16)
    values_here = jnp.dot(
        arrived, value_full.reshape(model, inner), preferred_element_type=jnp.float32
    ).astype(jnp.bfloat16)
    token_count = queries.shape[0]
    head_count = queries.shape[1] // HEAD
    query_heads = queries.reshape(token_count, head_count, HEAD)
    key_heads = keys_here.reshape(slots, head_count, HEAD)
    value_heads = values_here.reshape(slots, head_count, HEAD)
    score_scale = 1.0 / math.sqrt(HEAD)
    scores = (
        jnp.einsum("qhd,khd->hqk", query_heads, key_heads, preferred_element_type=jnp.float32)
        * score_scale
    )
    matching = dec_doc[:, None] == slot_docs[None, :]
    scores = jnp.where(matching[None, :, :], scores, -1e30)
    row_peak = jnp.max(scores, axis=2, keepdims=True)
    exponent = jnp.exp(scores - row_peak)
    probs = (exponent / jnp.sum(exponent, axis=2, keepdims=True)).astype(jnp.bfloat16)
    attended = jnp.einsum("hqk,khd->qhd", probs, value_heads, preferred_element_type=jnp.float32)
    attended = attended.astype(jnp.bfloat16).reshape(token_count, head_count * HEAD)
    partial_rows = jnp.einsum(
        "tk,skn->tsn", attended, out_full, preferred_element_type=jnp.float32
    ).reshape(token_count, shard_count * out_weight.shape[1])
    return lax.psum_scatter(
        partial_rows.astype(jnp.bfloat16), "tensor", scatter_dimension=1, tiled=True
    )


def solution(mesh):
    return jax.shard_map(
        on_device,
        mesh=mesh,
        in_specs=(
            P(("groups", "seq"), None),
            P(("groups", "seq")),
            P(("groups", "seq")),
            P(("groups", "seq")),
            P(("groups", "seq"), "tensor"),
            P("seq", "tensor"),
            P("seq", "tensor"),
            P("tensor", "seq"),
        ),
        out_specs=P(("groups", "seq"), "tensor"),
        check_vma=False,
    )
```

time: 464 us -> 318 us (0.69)
  waiting for transfers between devices: 301 us -> 7.02 us
  Pallas kernels: 0 us -> 244 us
  blocking collectives: 97 us -> 0 us
    all_gather x4 -> x0, waiting for transfers between devices: 293 us -> none  [the longest x2 200 us: gather_columns(): lax.all_gather(half_columns(weight), ('groups', 'seq'), axis=0, tiled=True)]
    pallas_call x0 -> x1, Pallas kernels: none -> 244 us  [exchange(): pl.pallas_call(functools.partial(exchange_kernel, shards, groups, tensors...]
    all_to_all x1 -> x0, blocking collectives: 66.7 us -> none  [on_device(): lax.all_to_all(packed, 'seq', split_axis=0, concat_axis=0, tiled=True)]
    all_gather x1 -> x0, blocking collectives: 30.4 us -> none  [on_device(): tags = lax.all_gather(jnp.stack([enc_owner, enc_doc]), 'seq', axis=0)]
    dot_general x0 -> x1, local copies, waits for them, and re-layouts: none -> 11.4 us  [on_device(): jnp.einsum('tk,skn->tsn', attended, out_full, preferred_element_type=jnp....]
    dot_general x6 -> x4, matrix products: 27.3 us -> 25.3 us  [the longest x1 10.8 us: on_device(): jnp.dot(arrived, key_full.reshape(model, inner), preferred_element_type=j...]
  transfers between devices with their start and end apart: 5 -> 1, of which waited for: 4 -> 1; matrix products, arithmetic and copies ran while one was open for 7% -> 0% of each run, Pallas kernels for 0% -> 0%
where the time goes in v2:
time: 318 us; the launch traced here: 317 us
  Pallas kernels  244 us (77%)
  matrix products  30.2 us (9%)
  local copies, waits for them, and re-layouts  17.9 us (6%)
  between operations  13.5 us (4%)
  waiting for transfers between devices  7.02 us (2%)
  other arithmetic  4.94 us (2%)
    pallas_call x1, Pallas kernels, exchange(): pl.pallas_call(functools.partial(exchange_kernel, shards, groups, tensors...  244 us
    dot_general x1, local copies, waits for them, and re-layouts, on_device(): jnp.einsum('tk,skn->tsn', attended, out_full, preferred_element_type=jnp....  11.4 us
    dot_general x1, matrix products, on_device(): jnp.dot(arrived, key_full.reshape(model, inner), preferred_element_type=j...  10.8 us
    dot_general x1, matrix products, on_device(): jnp.einsum('tk,skn->tsn', attended, out_full, preferred_element_type=jnp....  7.13 us
    reduce_scatter x1, waiting for transfers between devices, on_device(): lax.psum_scatter(partial_rows.astype(jnp.bfloat16), 'tensor', scatter_dim...  7 us
  transfers between devices with their start and end apart: 1, of which 1 were waited for; matrix products, arithmetic and copies ran while one was open for 0% of the time, Pallas kernels for 0%

profile of v2, /device:TPU:0, one launch (start us, length us, event | category | flops | bytes accessed | tf_op | source)
XLA Modules:
  0.0 317.2 jit_solution(12418988716088321632)
XLA Ops:
  6.5 0.0 reduce-scatter.2.cloned.1.call-start
  6.5 0.8 reshape.206
  7.3 0.6 fusion.32
  7.9 0.8 reshape.207
  8.7 1.3 iota_compare_fusion.2
  10.0 1.3 iota_compare_fusion
  11.2 1.4 fusion.31
  12.7 0.1 select_select_fusion.1
  12.7 2.2 select_select_fusion.x_ref
  14.9 0.6 broadcast_in_dim.158.d_ref
  15.5 243.6 %shard_map.82 = (bf16[8,80,4096]{2,1,0:T(8,128)(2,1)}, s32[8,8,128]{2,1,0:T(8,128)}, bf16[8,512,1024]{2,1,0:T(8,128)(2,1)}, bf16[8,512,1024]{2,1,0:T(8,128)(2,1)}, bf16[8,1024,512]{2,1,0:T(8,128)(2,1)}) custom-call(bf16[8,80,2048]{2,1,0:T(8,128)(2,1)} %select_select_fusion.x_ref, s32[8,8,128]{2,1,0:T(8,128)} %broadcast_in_dim.158.d_ref, ...), custom_call_target="tpu_custom_call" | custom-call | tf_op jit(solution)/shard_map/pallas_call | solution.py:231
  259.2 0.0 copy-start.2
  259.2 0.0 copy-start.3
  259.2 10.8 %convolution_convert_fusion.1 = bf16[640,1024]{1,0:T(8,128)(2,1)} fusion(bf16[640,4096]{1,0:T(8,128)(2,1)} %bitcast.68, bf16[4096,1024]{1,0:T(8,128)(2,1)} %bitcast.67), kind=kOutput, calls=%fused_computation.7 | convolution fusion | flops 5369364480 | bytes 14942208 | tf_op jit(solution)/shard_map/dot_general | solution.py:281
  269.9 0.0 copy-done.2
  269.9 0.0 copy-done.3
  269.9 5.6 %convolution_convert_fusion.2 = bf16[640,1024]{1,0:T(8,128)(2,1)S(1)} fusion(bf16[640,4096]{1,0:T(8,128)(2,1)S(1)} %bitcast.69, bf16[4096,1024]{1,0:T(8,128)(2,1)S(1)} %bitcast.66), kind=kOutput, calls=%fused_computation.8 | convolution fusion | flops 5369364480 | bytes 14942208 | tf_op jit(solution)/shard_map/dot_general | solution.py:284
  275.5 0.0 copy-start.1
  275.5 0.0 copy-start
  275.5 1.5 copy.19
  277.0 0.8 slice_reduce_fusion
  277.8 0.1 eq.84
  277.9 0.0 copy-done.1
  277.9 0.2 broadcast_compare_fusion
  278.0 0.0 copy-done
  278.0 1.9 fusion.2
  279.9 2.4 fusion.33
  282.3 11.4 %copy.17 = bf16[8,512,1024]{2,1,0:T(8,128)(2,1)} copy(bf16[8,512,1024]{1,2,0:T(8,128)(2,1)} %bitcast.59) | data formatting | bytes 16777216 | tf_op jit(solution)/shard_map/tk,skn->tsn/dot_general | solution.py:304
  293.7 2.4 fusion.9
  296.2 7.1 %convolution_convert_fusion = bf16[256,4096]{1,0:T(8,128)(2,1)} fusion(bf16[256,1024]{0,1:T(8,128)(2,1)S(1)} %bitcast.70, bf16[4096,1024]{1,0:T(8,128)(2,1)} %bitcast.60), kind=kOutput, calls=%fused_computation.1 | convolution fusion | flops 2148532224 | bytes 11010048 | tf_op jit(solution)/shard_map/tk,skn->tsn/dot_general | solution.py:304
  303.3 0.0 reduce-scatter.2.cloned.1.call-update
  303.3 7.0 %reduce-scatter.2.cloned.1.call-done = bf16[256,2048]{1,0:T(8,128)(2,1)} async-done(((bf16[256,4096]{1,0:T(8,128)(2,1)}), bf16[256,2048]{1,0:T(8,128)(2,1)}) %reduce-scatter.2.cloned.1.call-update) | async-done | bytes 1048592 | tf_op jit(solution)/shard_map/reduce_scatter | solution.py:307
  (1 shorter events, 0.0 us)
Async XLA Ops:
  6.5 303.8 %reduce-scatter.2.cloned.1.call-start = ((), (), s32[]{:S(2)}) async-start(), calls=%async_computation.1 | async-start | bytes 3145728 | tf_op jit(solution)/shard_map/reduce_scatter | solution.py:307
  259.2 10.8 %copy-start.2 = (bf16[8,512,1024]{2,1,0:T(8,128)(2,1)S(1)}, bf16[8,512,1024]{2,1,0:T(8,128)(2,1)}, u32[]{:S(2)}) copy-start(bf16[8,512,1024]{2,1,0:T(8,128)(2,1)} %get-tuple-element.11) | copy-start | bytes 25165828
  259.2 10.8 %copy-start.3 = (bf16[8,80,4096]{2,1,0:T(8,128)(2,1)S(1)}, bf16[8,80,4096]{2,1,0:T(8,128)(2,1)}, u32[]{:S(2)}) copy-start(bf16[8,80,4096]{2,1,0:T(8,128)(2,1)} %get-tuple-element.10) | copy-start | bytes 15728644
  275.5 2.3 copy-start.1
  275.5 2.5 copy-start
Sparse Core Ops, SparseCore 0:
  303.5 6.8 reduce-scatter.1

commit v3 on v2

--- a/solution.py
+++ b/solution.py
@@ -57,23 +57,6 @@
             device_id=device, device_id_type=MESH,
         )
 
-    for j in range(1, shards):
-        target = lax.rem(me + j, shards)
-
-        def rows_copy(target=target):
-            return remote(
-                x_ref.at[target], xg.at[me, :, columns],
-                x_send.at[target], x_recv.at[me], {"seq": target},
-            )
-
-        def docs_copy(target=target):
-            return remote(
-                d_ref.at[target], dg.at[me], d_send.at[target], d_recv.at[me], {"seq": target}
-            )
-
-        send(None, rows_copy)
-        send(None, docs_copy)
-
     weights = ((k_ref, kg, 1), (v_ref, vg, 1), (o_ref, og, 0))
 
     def piece_of(which, cross, owner):
@@ -123,11 +106,32 @@
     can_up = layer + 1 < layers
     can_down = layer >= 1
 
-    for which in range(3):
-        for cross in (0, 1):
+    def first(cross):
+        for which in range(3):
+            forward(None, which, cross, me, True, side_send, beside, group)
             forward(can_up, which, cross, me, True, up_send, up, group)
             forward(can_down, which, cross, me, True, down_send, down, group)
-            forward(None, which, cross, me, True, side_send, beside, group)
+
+    first(1)
+
+    for j in range(1, shards):
+        target = lax.rem(me + j, shards)
+
+        def rows_copy(target=target):
+            return remote(
+                x_ref.at[target], xg.at[me, :, columns],
+                x_send.at[target], x_recv.at[me], {"seq": target},
+            )
+
+        def docs_copy(target=target):
+            return remote(
+                d_ref.at[target], dg.at[me], d_send.at[target], d_recv.at[me], {"seq": target}
+            )
+
+        send(None, rows_copy)
+        send(None, docs_copy)
+
+    first(0)
 
     own_copies = [
         pltpu.make_async_copy(x_ref.at[me], xg.at[me, :, columns], local_sem.at[0]),
@@ -146,39 +150,35 @@
 
     send(None, own_rows)
 
-    def along(distance):
+    def along(distance, cross):
         for which in range(3):
-            for cross in (0, 1):
-                for sign in (-1, 1):
-                    there = layer + sign * distance
-                    origin = there * 2 + side
+            for sign in (-1, 1):
+                there = layer + sign * distance
+                origin = there * 2 + side
+                exists = there >= 0 if sign < 0 else there < layers
+                arrive(exists, which, cross, origin, group)
+                if cross:
+                    forward(exists, which, 1, origin, False, cross_send, to_group, group)
+                if sign < 0:
+                    forward(both(exists, can_up), which, cross, origin, False, up_send, up, group)
+                else:
+                    forward(
+                        both(exists, can_down), which, cross, origin, False,
+                        down_send, down, group,
+                    )
+                forward(exists, which, cross, origin, False, side_send, beside, group)
+
+    def across(distance, cross):
+        for which in range(3):
+            for sign in (-1, 1) if distance else (1,):
+                there = layer + sign * distance
+                origin = there * 2 + 1 - side
+                exists = None
+                if distance:
                     exists = there >= 0 if sign < 0 else there < layers
-                    arrive(exists, which, cross, origin, group)
-                    if sign < 0:
-                        forward(
-                            both(exists, can_up), which, cross, origin, False, up_send, up, group
-                        )
-                    else:
-                        forward(
-                            both(exists, can_down), which, cross, origin, False,
-                            down_send, down, group,
-                        )
-                    forward(exists, which, cross, origin, False, side_send, beside, group)
-                    if cross:
-                        forward(exists, which, 1, origin, False, cross_send, to_group, group)
-
-    def across(distance):
-        for which in range(3):
-            for cross in (0, 1):
-                for sign in (-1, 1) if distance else (1,):
-                    there = layer + sign * distance
-                    origin = there * 2 + 1 - side
-                    exists = None
-                    if distance:
-                        exists = there >= 0 if sign < 0 else there < layers
-                    arrive(exists, which, cross, origin, group)
-                    if cross:
-                        forward(exists, which, 1, origin, False, cross_send, to_group, group)
+                arrive(exists, which, cross, origin, group)
+                if cross:
+                    forward(exists, which, 1, origin, False, cross_send, to_group, group)
 
     def pass_rows():
         for j in range(1, shards):
@@ -196,12 +196,15 @@
 
             send(None, share)
 
-    across(0)
+    across(0, 1)
     for distance in range(1, layers):
-        along(distance)
-        across(distance)
-        if distance == 1:
+        along(distance, 1)
+        along(distance, 0)
+        across(distance, 1)
+        if distance == min(2, layers - 1):
             pass_rows()
+    for distance in range(layers):
+        across(distance, 0)
 
     others = pl.ds(pl.multiple_of((1 - core) * width, 128), width)
     for j in range(shards):
@@ -301,11 +304,15 @@
     probs = (exponent / jnp.sum(exponent, axis=2, keepdims=True)).astype(jnp.bfloat16)
     attended = jnp.einsum("hqk,khd->qhd", probs, value_heads, preferred_element_type=jnp.float32)
     attended = attended.astype(jnp.bfloat16).reshape(token_count, head_count * HEAD)
-    partial_rows = jnp.einsum(
-        "tk,skn->tsn", attended, out_full, preferred_element_type=jnp.float32
-    ).reshape(token_count, shard_count * out_weight.shape[1])
+    partial_rows = jnp.concatenate(
+        [
+            jnp.dot(attended, out_full[s], preferred_element_type=jnp.float32).astype(jnp.bfloat16)
+            for s in range(shard_count)
+        ],
+        axis=1,
+    )
     return lax.psum_scatter(
-        partial_rows.astype(jnp.bfloat16), "tensor", scatter_dimension=1, tiled=True
+        partial_rows, "tensor", scatter_dimension=1, tiled=True
     )
 
 

time: 318 us -> 294 us (0.925)
  Pallas kernels: 244 us -> 223 us
  local copies, waits for them, and re-layouts: 17.9 us -> 7.83 us
  matrix products: 30.2 us -> 37.5 us
    pallas_call x1, Pallas kernels: 244 us -> 223 us  [exchange(): pl.pallas_call(functools.partial(exchange_kernel, shards, groups, tensors...]
    dot_general x1 -> x0, local copies, waits for them, and re-layouts: 11.4 us -> none  [on_device(): jnp.einsum('tk,skn->tsn', attended, out_full, preferred_element_type=jnp....]
    dot_general x1 -> x8, matrix products: 7.13 us -> 13.6 us  [on_device(): jnp.dot(attended, out_full[s], preferred_element_type=jnp.float32)]
where the time goes in v3:
time: 294 us; the launch traced here: 293 us
  Pallas kernels  223 us (76%)
  matrix products  37.5 us (13%)
  between operations  13.6 us (5%)
  local copies, waits for them, and re-layouts  7.83 us (3%)
  waiting for transfers between devices  6.34 us (2%)
  other arithmetic  4.87 us (2%)
    pallas_call x1, Pallas kernels, exchange(): pl.pallas_call(functools.partial(exchange_kernel, shards, groups, tensors...  223 us
    dot_general x8, matrix products, on_device(): jnp.dot(attended, out_full[s], preferred_element_type=jnp.float32)  13.6 us
    dot_general x1, matrix products, on_device(): jnp.dot(arrived, key_full.reshape(model, inner), preferred_element_type=j...  10.8 us
    reduce_scatter x1, waiting for transfers between devices, on_device(): lax.psum_scatter(partial_rows, 'tensor', scatter_dimension=1, tiled=True)  6.33 us
  transfers between devices with their start and end apart: 1, of which 1 were waited for; matrix products, arithmetic and copies ran while one was open for 0% of the time, Pallas kernels for 0%

profile of v3, /device:TPU:0, one launch (start us, length us, event | category | flops | bytes accessed | tf_op | source)
XLA Modules:
  0.0 293.3 jit_solution(621647282503545221)
XLA Ops:
  6.5 0.0 reduce-scatter.2.cloned.1.call-start
  6.5 0.8 reshape.204
  7.3 0.6 fusion.56
  7.9 0.8 reshape.205
  8.7 1.3 iota_compare_fusion.2
  10.0 1.2 iota_compare_fusion
  11.2 1.4 fusion.55
  12.5 0.1 select_select_fusion.1
  12.6 2.2 select_select_fusion.x_ref
  14.8 0.6 broadcast_in_dim.158.d_ref
  15.4 223.2 %shard_map.82 = (bf16[8,80,4096]{2,1,0:T(8,128)(2,1)}, s32[8,8,128]{2,1,0:T(8,128)}, bf16[8,512,1024]{2,1,0:T(8,128)(2,1)}, bf16[8,512,1024]{2,1,0:T(8,128)(2,1)}, bf16[8,1024,512]{2,1,0:T(8,128)(2,1)}) custom-call(bf16[8,80,2048]{2,1,0:T(8,128)(2,1)} %select_select_fusion.x_ref, s32[8,8,128]{2,1,0:T(8,128)} %broadcast_in_dim.158.d_ref, ...), custom_call_target="tpu_custom_call" | custom-call | tf_op jit(solution)/shard_map/pallas_call | solution.py:234
  238.6 0.0 copy-start.3
  238.6 0.0 copy-start.4
  238.6 10.8 %convolution_convert_fusion = bf16[640,1024]{1,0:T(8,128)(2,1)} fusion(bf16[640,4096]{1,0:T(8,128)(2,1)} %bitcast.94, bf16[4096,1024]{1,0:T(8,128)(2,1)} %bitcast.93), kind=kOutput, calls=%fused_computation.6 | convolution fusion | flops 5369364480 | bytes 14942208 | tf_op jit(solution)/shard_map/dot_general | solution.py:284
  249.4 0.0 copy-done.3
  249.4 0.0 copy-done.4
  249.4 5.6 %convolution_convert_fusion.1 = bf16[640,1024]{1,0:T(8,128)(2,1)S(1)} fusion(bf16[640,4096]{1,0:T(8,128)(2,1)S(1)} %bitcast.95, bf16[4096,1024]{1,0:T(8,128)(2,1)S(1)} %bitcast.92), kind=kOutput, calls=%fused_computation.7 | convolution fusion | flops 5369364480 | bytes 14942208 | tf_op jit(solution)/shard_map/dot_general | solution.py:287
  255.0 0.0 copy-start.2
  255.0 0.0 copy-start.1
  255.0 1.5 copy.14
  256.5 0.8 slice_reduce_fusion
  257.3 0.1 eq.84
  257.4 0.0 copy-done.2
  257.4 0.2 broadcast_compare_fusion
  257.5 0.0 copy-done.1
  257.5 1.9 fusion.2
  259.4 2.4 fusion.57
  261.8 3.2 %fusion.9 = bf16[4,256,256]{2,1,0:T(8,128)(2,1)} fusion(bf16[640,4,256]{0,2,1:T(8,128)(2,1)} %bitcast.87, f32[4,256]{1,0:T(4,128)S(1)} %fusion.57, f32[4,640,256]{2,1,0:T(8,128)S(1)} %fusion.2, pred[256,640]{0,1:T(8,128)(4,1)S(1)} %broadcast_compare_fusion), kind=kOutput, calls=%fused_computation.15 | convolution fusion | flops 339084928 | bytes 4624384 | tf_op jit(solution)/shard_map/hqk,khd->qhd/dot_general | solution.py:305
  265.1 0.0 copy-start.5
  265.1 1.9 fusion.17
  267.0 0.0 copy-done.5
  267.0 1.7 fusion.16
  268.7 1.7 fusion.15
  270.3 1.7 fusion.14
  272.0 1.7 fusion.13
  273.7 1.7 fusion.12
  275.4 1.7 fusion.11
  277.1 1.7 fusion.10
  278.8 0.0 copy-start
  278.8 1.3 copy-done
  280.1 0.0 reduce-scatter.2.cloned.1.call-update
  280.1 6.3 %reduce-scatter.2.cloned.1.call-done = bf16[256,2048]{1,0:T(8,128)(2,1)} async-done(((bf16[256,4096]{1,0:T(8,128)(2,1)}), bf16[256,2048]{1,0:T(8,128)(2,1)}) %reduce-scatter.2.cloned.1.call-update) | async-done | bytes 1048592 | tf_op jit(solution)/shard_map/reduce_scatter | solution.py:314
  (1 shorter events, 0.0 us)
Async XLA Ops:
  6.5 279.9 %reduce-scatter.2.cloned.1.call-start = ((), (), s32[]{:S(2)}) async-start(), calls=%async_computation.1 | async-start | bytes 3145728 | tf_op jit(solution)/shard_map/reduce_scatter | solution.py:314
  238.6 10.8 %copy-start.3 = (bf16[8,512,1024]{2,1,0:T(8,128)(2,1)S(1)}, bf16[8,512,1024]{2,1,0:T(8,128)(2,1)}, u32[]{:S(2)}) copy-start(bf16[8,512,1024]{2,1,0:T(8,128)(2,1)} %get-tuple-element.11) | copy-start | bytes 25165828
  238.6 10.8 %copy-start.4 = (bf16[8,80,4096]{2,1,0:T(8,128)(2,1)S(1)}, bf16[8,80,4096]{2,1,0:T(8,128)(2,1)}, u32[]{:S(2)}) copy-start(bf16[8,80,4096]{2,1,0:T(8,128)(2,1)} %get-tuple-element.10) | copy-start | bytes 15728644
  255.0 2.4 copy-start.2
  255.0 2.5 copy-start.1
  265.1 1.9 copy-start.5
  278.8 1.3 copy-start
Sparse Core Ops, SparseCore 0:
  280.3 6.1 reduce-scatter.1

commit v4 on v3

--- a/solution.py
+++ b/solution.py
@@ -249,6 +249,90 @@
         + [dma((9 * shards,))],
         compiler_params=pltpu.CompilerParams(collective_id=0, has_side_effects=True),
     )(rows, docs, key_weight, value_weight, out_weight)
+
+
+def attend_kernel(
+    steps, x_ref, k_ref, v_ref, q_ref, dec_ref, docs_ref, o_ref, out_ref,
+    key_sums, value_sums, attended,
+):
+    step = pl.program_id(0)
+
+    @pl.when(step == 0)
+    def _():
+        key_sums[...] = jnp.zeros_like(key_sums)
+        value_sums[...] = jnp.zeros_like(value_sums)
+
+    @pl.when(step < steps)
+    def _():
+        rows = x_ref[...]
+        key_sums[...] += jnp.dot(rows, k_ref[...], preferred_element_type=jnp.float32)
+        value_sums[...] += jnp.dot(rows, v_ref[...], preferred_element_type=jnp.float32)
+
+    @pl.when(step == steps - 1)
+    def _():
+        matching = dec_ref[...] == docs_ref[...]
+        for head in range(q_ref.shape[1] // HEAD):
+            cut = slice(head * HEAD, (head + 1) * HEAD)
+            scores = lax.dot_general(
+                q_ref[:, cut], key_sums[:, cut].astype(jnp.bfloat16),
+                (((1,), (1,)), ((), ())), preferred_element_type=jnp.float32,
+            )
+            scores = jnp.where(matching, scores * (1.0 / math.sqrt(HEAD)), -1e30)
+            exponent = jnp.exp(scores - jnp.max(scores, axis=1, keepdims=True))
+            probs = (exponent / jnp.sum(exponent, axis=1, keepdims=True)).astype(jnp.bfloat16)
+            attended[:, cut] = jnp.dot(
+                probs, value_sums[:, cut].astype(jnp.bfloat16),
+                preferred_element_type=jnp.float32,
+            ).astype(jnp.bfloat16)
+
+    @pl.when(step >= steps)
+    def _():
+        width = o_ref.shape[2]
+        for shard in range(o_ref.shape[0]):
+            out_ref[:, shard * width : (shard + 1) * width] = jnp.dot(
+                attended[...], o_ref[shard], preferred_element_type=jnp.float32
+            ).astype(jnp.bfloat16)
+
+
+def attend(rows, key_full, value_full, queries, dec_doc, slot_docs, out_full):
+    slots, model = rows.shape
+    inner = key_full.shape[1]
+    tokens = queries.shape[0]
+    shards, _, width = out_full.shape
+    block = 512
+    steps = model // block
+    per_block = block // width
+
+    def project_step(i):
+        return jnp.minimum(i, steps - 1)
+
+    def output_step(i):
+        return jnp.maximum(i - steps, 0)
+
+    def whole(shape):
+        return pl.BlockSpec(shape, lambda i: (0, 0))
+
+    return pl.pallas_call(
+        functools.partial(attend_kernel, steps),
+        grid=(steps + shards // per_block,),
+        out_shape=jax.ShapeDtypeStruct((tokens, shards * width), jnp.bfloat16),
+        in_specs=[
+            pl.BlockSpec((slots, block), lambda i: (0, project_step(i))),
+            pl.BlockSpec((block, inner), lambda i: (project_step(i), 0)),
+            pl.BlockSpec((block, inner), lambda i: (project_step(i), 0)),
+            whole(queries.shape),
+            whole(dec_doc.shape),
+            whole(slot_docs.shape),
+            pl.BlockSpec((per_block, inner, width), lambda i: (output_step(i), 0, 0)),
+        ],
+        out_specs=pl.BlockSpec((tokens, block), lambda i: (0, output_step(i))),
+        scratch_shapes=[
+            pltpu.VMEM((slots, inner), jnp.float32),
+            pltpu.VMEM((slots, inner), jnp.float32),
+            pltpu.VMEM((tokens, inner), jnp.bfloat16),
+        ],
+        compiler_params=pltpu.CompilerParams(vmem_limit_bytes=40 * 1024 * 1024),
+    )(rows, key_full, value_full, queries, dec_doc, slot_docs, out_full)
 
 
 def on_device(enc_rows, enc_owner, enc_doc, dec_doc, queries, key_weight, value_weight, out_weight):
@@ -278,38 +362,14 @@
         packed, packed_docs, key_weight, value_weight, out_weight
     )
     slots = shard_count * slot
-    arrived = arrived.reshape(slots, model)
-    slot_docs = slot_docs[:, 0, :slot].reshape(slots)
-    inner = key_weight.shape[1]
-    keys_here = jnp.dot(
-        arrived, key_full.reshape(model, inner), preferred_element_type=jnp.float32
-    ).astype(jnp.bfloat16)
-    values_here = jnp.dot(
-        arrived, value_full.reshape(model, inner), preferred_element_type=jnp.float32
-    ).astype(jnp.bfloat16)
-    token_count = queries.shape[0]
-    head_count = queries.shape[1] // HEAD
-    query_heads = queries.reshape(token_count, head_count, HEAD)
-    key_heads = keys_here.reshape(slots, head_count, HEAD)
-    value_heads = values_here.reshape(slots, head_count, HEAD)
-    score_scale = 1.0 / math.sqrt(HEAD)
-    scores = (
-        jnp.einsum("qhd,khd->hqk", query_heads, key_heads, preferred_element_type=jnp.float32)
-        * score_scale
-    )
-    matching = dec_doc[:, None] == slot_docs[None, :]
-    scores = jnp.where(matching[None, :, :], scores, -1e30)
-    row_peak = jnp.max(scores, axis=2, keepdims=True)
-    exponent = jnp.exp(scores - row_peak)
-    probs = (exponent / jnp.sum(exponent, axis=2, keepdims=True)).astype(jnp.bfloat16)
-    attended = jnp.einsum("hqk,khd->qhd", probs, value_heads, preferred_element_type=jnp.float32)
-    attended = attended.astype(jnp.bfloat16).reshape(token_count, head_count * HEAD)
-    partial_rows = jnp.concatenate(
-        [
-            jnp.dot(attended, out_full[s], preferred_element_type=jnp.float32).astype(jnp.bfloat16)
-            for s in range(shard_count)
-        ],
-        axis=1,
+    partial_rows = attend(
+        arrived.reshape(slots, model),
+        key_full.reshape(model, key_weight.shape[1]),
+        value_full.reshape(model, value_weight.shape[1]),
+        queries,
+        dec_doc[:, None],
+        slot_docs[:, 0, :slot].reshape(1, slots),
+        out_full,
     )
     return lax.psum_scatter(
         partial_rows, "tensor", scatter_dimension=1, tiled=True

time: 294 us -> 281 us (0.956)
  matrix products: 37.5 us -> 0 us
  Pallas kernels: 223 us -> 248 us
    dot_general x12 -> x0, matrix products: 35 us -> none  [the longest x8 13.6 us: on_device(): jnp.dot(attended, out_full[s], preferred_element_type=jnp.float32)]
    pallas_call x0 -> x1, Pallas kernels: none -> 24.7 us  [attend(): pl.pallas_call(functools.partial(attend_kernel, steps), grid=(steps + sha...]
where the time goes in v4:
time: 281 us; the launch traced here: 280 us
  Pallas kernels  248 us (88%)
  between operations  13.5 us (5%)
  local copies, waits for them, and re-layouts  7.65 us (3%)
  waiting for transfers between devices  6.34 us (2%)
  other arithmetic  4.81 us (2%)
    pallas_call x1, Pallas kernels, exchange(): pl.pallas_call(functools.partial(exchange_kernel, shards, groups, tensors...  223 us
    pallas_call x1, Pallas kernels, attend(): pl.pallas_call(functools.partial(attend_kernel, steps), grid=(steps + sha...  24.7 us
    reduce_scatter x1, waiting for transfers between devices, on_device(): lax.psum_scatter(partial_rows, 'tensor', scatter_dimension=1, tiled=True)  6.33 us
  transfers between devices with their start and end apart: 1, of which 1 were waited for; matrix products, arithmetic and copies ran while one was open for 0% of the time, Pallas kernels for 0%

profile of v4, /device:TPU:0, one launch (start us, length us, event | category | flops | bytes accessed | tf_op | source)
XLA Modules:
  0.0 280.2 jit_solution(4975858909788511501)
XLA Ops:
  6.5 0.0 reduce-scatter.2.cloned.1.call-start
  6.5 0.8 reshape.160
  7.3 0.6 fusion.5
  7.9 0.8 reshape.161
  8.7 1.3 iota_compare_fusion.2
  10.0 1.3 iota_compare_fusion
  11.3 1.4 fusion.4
  12.7 2.2 select_select_fusion.x_ref
  14.8 0.1 select_select_fusion.1
  14.9 0.6 broadcast_in_dim.145.d_ref
  15.5 0.0 copy-start.2
  15.5 0.0 copy-start.1
  15.5 223.2 %shard_map.82 = (bf16[8,80,4096]{2,1,0:T(8,128)(2,1)}, s32[8,8,128]{2,1,0:T(8,128)}, bf16[8,512,1024]{2,1,0:T(8,128)(2,1)}, bf16[8,512,1024]{2,1,0:T(8,128)(2,1)}, bf16[8,1024,512]{2,1,0:T(8,128)(2,1)}) custom-call(bf16[8,80,2048]{2,1,0:T(8,128)(2,1)} %select_select_fusion.x_ref, s32[8,8,128]{2,1,0:T(8,128)} %broadcast_in_dim.145.d_ref, ...), custom_call_target="tpu_custom_call" | custom-call | tf_op jit(solution)/shard_map/pallas_call | solution.py:234
  238.8 0.8 slice_reduce_fusion
  239.6 0.1 reshape_squeeze.3.docs_ref
  239.6 0.0 copy-done.2
  239.7 0.1 copy.9.dec_ref
  239.8 0.0 copy-done.1
  239.8 0.0 copy-start
  239.8 2.5 copy-done
  242.3 24.7 %shard_map.83 = bf16[256,4096]{1,0:T(8,128)(2,1)} custom-call(bf16[640,4096]{1,0:T(8,128)(2,1)S(1)} %bitcast.16, bf16[4096,1024]{1,0:T(8,128)(2,1)} %bitcast.17, bf16[4096,1024]{1,0:T(8,128)(2,1)} %bitcast.18, bf16[256,1024]{1,0:T(8,128)(2,1)S(1)} %copy-done.1, s32[256,1]{1,0:T(8,128)S(1)} %copy.9.dec_ref, s32[1,640]{1,0:T(1,128)S(1)} %reshape_squeeze.3.docs_ref, ...), custom_call_target="tpu_custom_call" | custom-call | tf_op jit(solution)/shard_map/pallas_call | solution.py:315
  267.0 0.0 reduce-scatter.2.cloned.1.call-update
  267.1 6.3 %reduce-scatter.2.cloned.1.call-done = bf16[256,2048]{1,0:T(8,128)(2,1)} async-done(((bf16[256,4096]{1,0:T(8,128)(2,1)}), bf16[256,2048]{1,0:T(8,128)(2,1)}) %reduce-scatter.2.cloned.1.call-update) | async-done | bytes 1048592 | tf_op jit(solution)/shard_map/reduce_scatter | solution.py:374
  (1 shorter events, 0.0 us)
Async XLA Ops:
  6.5 266.9 %reduce-scatter.2.cloned.1.call-start = ((), (), s32[]{:S(2)}) async-start(), calls=%async_computation.1 | async-start | bytes 3145728 | tf_op jit(solution)/shard_map/reduce_scatter | solution.py:374
  15.5 224.1 %copy-start.2 = (s32[256]{0:T(256)S(1)}, s32[256]{0:T(256)}, u32[]{:S(2)}) copy-start(s32[256]{0:T(256)} %param.11) | copy-start | bytes 3076
  15.5 224.3 %copy-start.1 = (bf16[256,1024]{1,0:T(8,128)(2,1)S(1)}, bf16[256,1024]{1,0:T(8,128)(2,1)}, u32[]{:S(2)}) copy-start(bf16[256,1024]{1,0:T(8,128)(2,1)} %q_ref.1) | copy-start | bytes 1572868
  239.8 2.5 copy-start
Sparse Core Ops, SparseCore 0:
  267.2 6.1 reduce-scatter.1

commit v5 on v4

--- a/solution.py
+++ b/solution.py
@@ -113,23 +113,6 @@
             forward(can_down, which, cross, me, True, down_send, down, group)
 
     first(1)
-
-    for j in range(1, shards):
-        target = lax.rem(me + j, shards)
-
-        def rows_copy(target=target):
-            return remote(
-                x_ref.at[target], xg.at[me, :, columns],
-                x_send.at[target], x_recv.at[me], {"seq": target},
-            )
-
-        def docs_copy(target=target):
-            return remote(
-                d_ref.at[target], dg.at[me], d_send.at[target], d_recv.at[me], {"seq": target}
-            )
-
-        send(None, rows_copy)
-        send(None, docs_copy)
 
     first(0)
 
@@ -180,6 +163,24 @@
                 if cross:
                     forward(exists, which, 1, origin, False, cross_send, to_group, group)
 
+    def send_rows():
+        for j in range(1, shards):
+            target = lax.rem(me + j, shards)
+
+            def rows_copy(target=target):
+                return remote(
+                    x_ref.at[target], xg.at[me, :, columns],
+                    x_send.at[target], x_recv.at[me], {"seq": target},
+                )
+
+            def docs_copy(target=target):
+                return remote(
+                    d_ref.at[target], dg.at[me], d_send.at[target], d_recv.at[me], {"seq": target}
+                )
+
+            send(None, rows_copy)
+            send(None, docs_copy)
+
     def pass_rows():
         for j in range(1, shards):
             source = lax.rem(me + shards - j, shards)
@@ -201,8 +202,9 @@
         along(distance, 1)
         along(distance, 0)
         across(distance, 1)
-        if distance == min(2, layers - 1):
-            pass_rows()
+        if distance == 1:
+            send_rows()
+    pass_rows()
     for distance in range(layers):
         across(distance, 0)
 

time: 281 us -> 280 us (level)
  Pallas kernels: 248 us -> 238 us
  waiting for transfers between devices: 6.34 us -> 15 us
    pallas_call x1, Pallas kernels: 223 us -> 214 us  [exchange(): pl.pallas_call(functools.partial(exchange_kernel, shards, groups, tensors...]
    reduce_scatter x1, waiting for transfers between devices: 6.33 us -> 15 us  [on_device(): lax.psum_scatter(partial_rows, 'tensor', scatter_dimension=1, tiled=True)]
where the time goes in v5:
time: 280 us; the launch traced here: 279 us
  Pallas kernels  238 us (85%)
  waiting for transfers between devices  15 us (5%)
  between operations  13.5 us (5%)
  local copies, waits for them, and re-layouts  7.65 us (3%)
  other arithmetic  4.81 us (2%)
    pallas_call x1, Pallas kernels, exchange(): pl.pallas_call(functools.partial(exchange_kernel, shards, groups, tensors...  214 us
    pallas_call x1, Pallas kernels, attend(): pl.pallas_call(functools.partial(attend_kernel, steps), grid=(steps + sha...  24.7 us
    reduce_scatter x1, waiting for transfers between devices, on_device(): lax.psum_scatter(partial_rows, 'tensor', scatter_dimension=1, tiled=True)  15 us
  transfers between devices with their start and end apart: 1, of which 1 were waited for; matrix products, arithmetic and copies ran while one was open for 0% of the time, Pallas kernels for 0%

profile of v5, /device:TPU:0, one launch (start us, length us, event | category | flops | bytes accessed | tf_op | source)
XLA Modules:
  0.0 279.3 jit_solution(3720263724448594570)
XLA Ops:
  6.5 0.0 reduce-scatter.2.cloned.1.call-start
  6.5 0.8 reshape.160
  7.3 0.6 fusion.5
  7.9 0.8 reshape.161
  8.7 1.3 iota_compare_fusion.2
  10.0 1.3 iota_compare_fusion
  11.3 1.4 fusion.4
  12.7 2.2 select_select_fusion.x_ref
  14.8 0.1 select_select_fusion.1
  14.9 0.6 broadcast_in_dim.145.d_ref
  15.5 0.0 copy-start.2
  15.5 0.0 copy-start.1
  15.5 213.6 %shard_map.82 = (bf16[8,80,4096]{2,1,0:T(8,128)(2,1)}, s32[8,8,128]{2,1,0:T(8,128)}, bf16[8,512,1024]{2,1,0:T(8,128)(2,1)}, bf16[8,512,1024]{2,1,0:T(8,128)(2,1)}, bf16[8,1024,512]{2,1,0:T(8,128)(2,1)}) custom-call(bf16[8,80,2048]{2,1,0:T(8,128)(2,1)} %select_select_fusion.x_ref, s32[8,8,128]{2,1,0:T(8,128)} %broadcast_in_dim.145.d_ref, ...), custom_call_target="tpu_custom_call" | custom-call | tf_op jit(solution)/shard_map/pallas_call | solution.py:236
  229.2 0.8 slice_reduce_fusion
  230.0 0.1 reshape_squeeze.3.docs_ref
  230.0 0.0 copy-done.2
  230.1 0.1 copy.9.dec_ref
  230.2 0.0 copy-done.1
  230.2 0.0 copy-start
  230.2 2.5 copy-done
  232.7 24.7 %shard_map.83 = bf16[256,4096]{1,0:T(8,128)(2,1)} custom-call(bf16[640,4096]{1,0:T(8,128)(2,1)S(1)} %bitcast.16, bf16[4096,1024]{1,0:T(8,128)(2,1)} %bitcast.17, bf16[4096,1024]{1,0:T(8,128)(2,1)} %bitcast.18, bf16[256,1024]{1,0:T(8,128)(2,1)S(1)} %copy-done.1, s32[256,1]{1,0:T(8,128)S(1)} %copy.9.dec_ref, s32[1,640]{1,0:T(1,128)S(1)} %reshape_squeeze.3.docs_ref, ...), custom_call_target="tpu_custom_call" | custom-call | tf_op jit(solution)/shard_map/pallas_call | solution.py:317
  257.4 0.0 reduce-scatter.2.cloned.1.call-update
  257.5 15.0 %reduce-scatter.2.cloned.1.call-done = bf16[256,2048]{1,0:T(8,128)(2,1)} async-done(((bf16[256,4096]{1,0:T(8,128)(2,1)}), bf16[256,2048]{1,0:T(8,128)(2,1)}) %reduce-scatter.2.cloned.1.call-update) | async-done | bytes 1048592 | tf_op jit(solution)/shard_map/reduce_scatter | solution.py:376
  (1 shorter events, 0.0 us)
Async XLA Ops:
  6.5 265.9 %reduce-scatter.2.cloned.1.call-start = ((), (), s32[]{:S(2)}) async-start(), calls=%async_computation.1 | async-start | bytes 3145728 | tf_op jit(solution)/shard_map/reduce_scatter | solution.py:376
  15.5 214.5 %copy-start.2 = (s32[256]{0:T(256)S(1)}, s32[256]{0:T(256)}, u32[]{:S(2)}) copy-start(s32[256]{0:T(256)} %param.11) | copy-start | bytes 3076
  15.5 214.7 %copy-start.1 = (bf16[256,1024]{1,0:T(8,128)(2,1)S(1)}, bf16[256,1024]{1,0:T(8,128)(2,1)}, u32[]{:S(2)}) copy-start(bf16[256,1024]{1,0:T(8,128)(2,1)} %q_ref.1) | copy-start | bytes 1572868
  230.2 2.5 copy-start
Sparse Core Ops, SparseCore 0:
  257.6 14.8 reduce-scatter.1
